TPU v7x, 128 devices: a whole 4x4x4 slice. The times are simulated.
128 devices in a mesh: section: 32 (over z, y, core), tensor: 4 (over x).
Axes of the slice: x: 4, y: 4, z: 4, core: 2. Of those that a mesh axis runs over, the one named last changes fastest.
Arguments:
- flight_state: bfloat16 [32, 512, 3584], P('section', 'tensor'), may hold values from -6 to 6
- flight_tokens: int32 [32, 3], P('section'), may hold values from 1 to 256, as said below
- flight_lists: int32 [32, 3], P('section'), may hold values from 0 to 1023, as said below
- incoming: bfloat16 [2, 512, 3584], P(None, 'tensor'), may hold values from -6 to 6
- incoming_tokens: int32 [2, 3], replicated, may hold values from 1 to 256, as said below
- norm_gain: float32 [32, 3584], P('section'), may hold values from 0.25 to 1.75
- query_weight: bfloat16 [32, 3584, 3584], P('section', None, 'tensor'), may hold values from -0.09375 to 0.09375
- query_bias: float32 [32, 3584], P('section', 'tensor'), may hold values from -10 to 10
- key_weight: bfloat16 [32, 3584, 512], P('section', None, 'tensor'), may hold values from -0.09375 to 0.09375
- key_bias: float32 [32, 512], P('section', 'tensor'), may hold values from -10 to 10
- value_weight: bfloat16 [32, 3584, 512], P('section', None, 'tensor'), may hold values from -0.09375 to 0.09375
- value_bias: float32 [32, 512], P('section', 'tensor'), may hold values from -3 to 3
- output_weight: bfloat16 [32, 3584, 3584], P('section', 'tensor'), may hold values from -0.09375 to 0.09375
- list_rows: int32 [1024], replicated, may hold values from 0 to 1023, each once
Outputs:
- next_state: bfloat16 [32, 512, 3584], P('section', 'tensor')
- list_sums: float32 [1024, 3584], P(('section', 'tensor'))
Inputs may be any that keep to these rules, and one draw needn't show every extreme that they name: `flight_tokens`: in each micro-batch the blocks ceil(tokens / 128) of its 3 programs sum to 4; in every draw some program has the most and some program has 1 token. `incoming_tokens`: in each micro-batch the blocks ceil(tokens / 128) of its 3 programs sum to 4; in every draw some program has the most and some program has 1 token. `flight_lists`: every micro-batch after the first gives one of its programs the list of some program of the micro-batch before it.
All inputs are finite; a program needn't handle non-finite values.
Results may differ from a plain program's by a relative error of at most 0.034.
Values may be sent and summed in bfloat16 or wider, within the bound.
A program may use at most 128 MiB of HBM per device.

v0:
```python
import math
import jax
import jax.numpy as jnp
from jax import lax
from jax.sharding import PartitionSpec as P

HEAD = 128
LAYERS = 28
BLOCK = 128
EPS = 1e-06
THETA = 1000000.0


def from_behind(block, axis, distance):
    devices = range(lax.axis_size(axis))
    route = [((i - distance) % len(devices), i) for i in devices]
    return lax.ppermute(block, axis, route)


def broadcast(value, axis, root):
    mine = lax.axis_index(axis) == root
    return lax.psum(jnp.where(mine, value, jnp.zeros_like(value)), axis)


def as_sent(value):
    return jax.tree.map(lambda a: a.astype(jnp.bfloat16) if a.dtype == jnp.float32 else a, value)


def row_layout(tokens, first, count):
    blocks = (tokens + BLOCK - 1) // BLOCK
    ends = (jnp.cumsum(blocks) * BLOCK).astype(jnp.int32)
    starts = ends - blocks * BLOCK
    slots = first + jnp.arange(count, dtype=jnp.int32)
    program = jnp.sum((slots[:, None] >= ends[None, :]).astype(jnp.int32), axis=1)
    chosen = program[:, None] == jnp.arange(tokens.shape[0], dtype=jnp.int32)[None, :]
    begin = jnp.sum(jnp.where(chosen, starts[None, :], 0), axis=1)
    length = jnp.sum(jnp.where(chosen, tokens[None, :], 0), axis=1)
    position = slots - begin
    return (program, position, position < length)


def rotate(values, position):
    half = values.shape[-1] // 2
    freq = THETA ** (-jnp.arange(half, dtype=jnp.float32) * 2.0 / values.shape[-1])
    angle = position.astype(jnp.float32)[:, None] * freq[None, :]
    cosine = jnp.cos(angle)[:, None, :]
    sine = jnp.sin(angle)[:, None, :]
    first_half = values[..., :half]
    second_half = values[..., half:]
    return jnp.concatenate(
        [first_half * cosine - second_half * sine, second_half * cosine + first_half * sine],
        axis=-1,
    )


def attend(queries, key_rows, value_rows, program, valid):
    total = queries.shape[0]
    width = min(512, total)
    scale = 1.0 / math.sqrt(queries.shape[-1])

    def one_block(index):
        scores = (
            jnp.einsum("qcgd,kcd->cgqk", queries, key_rows, preferred_element_type=jnp.float32)
            * scale
        )
        allowed = (program[:, None] == program[None, :]) & valid[None, :]
        scores = jnp.where(allowed[None, None], scores, -1e30)
        top = jnp.max(scores, axis=-1, keepdims=True)
        expo = jnp.exp(scores - top)
        probs = (expo / jnp.sum(expo, axis=-1, keepdims=True)).astype(jnp.bfloat16)
        mixed = jnp.einsum("cgqk,kcd->qcgd", probs, value_rows, preferred_element_type=jnp.float32)
        return mixed.astype(jnp.bfloat16)

    blocks = lax.map(one_block, jnp.arange(total // width, dtype=jnp.int32))
    return blocks.reshape(total, -1)


def normalize(state, gain):
    values = state.astype(jnp.float32)
    return (
        values * lax.rsqrt(jnp.mean(values * values, axis=-1, keepdims=True) + EPS) * gain
    ).astype(jnp.bfloat16)


def local(
    flight_state,
    flight_tokens,
    flight_lists,
    incoming,
    incoming_tokens,
    norm_gain,
    query_weight,
    query_bias,
    key_weight,
    key_bias,
    value_weight,
    value_bias,
    output_weight,
    list_rows,
):
    tensor_count = lax.axis_size("tensor")
    section_count = lax.axis_size("section")
    tensor_rank = lax.axis_index("tensor")
    section_rank = lax.axis_index("section")
    is_last = section_rank == section_count - 1
    active = section_rank < min(section_count, LAYERS)
    own_rows = flight_state.shape[1]
    all_rows = own_rows * tensor_count
    row_first = tensor_rank * own_rows
    query_cols = query_weight.shape[2]
    key_cols = key_weight.shape[2]
    kv_local = key_cols // HEAD
    groups = query_cols // key_cols
    gain = norm_gain[0]
    prog_count = flight_tokens.shape[1]

    def assemble(rows):
        return lax.all_gather(rows, "tensor", axis=0, tiled=True)

    tokens = flight_tokens[0]
    lists = flight_lists[0]
    part_list = []
    token_list = []
    lists_list = []
    whole = assemble(flight_state[0])
    for tick in range(incoming.shape[0]):
        piece = normalize(whole, gain)
        combined = jnp.concatenate(
            [
                jnp.dot(piece, query_weight[0], preferred_element_type=jnp.float32),
                jnp.dot(piece, key_weight[0], preferred_element_type=jnp.float32),
                jnp.dot(piece, value_weight[0], preferred_element_type=jnp.float32),
            ],
            axis=1,
        )
        heads_program, heads_position, heads_valid = row_layout(tokens, 0, all_rows)
        query_f = combined[:, :query_cols] + query_bias[0]
        key_f = combined[:, query_cols : query_cols + key_cols] + key_bias[0]
        value_f = combined[:, query_cols + key_cols :] + value_bias[0]
        queries = rotate(query_f.reshape(all_rows, kv_local * groups, HEAD), heads_position).astype(
            jnp.bfloat16
        )
        queries = queries.reshape(all_rows, kv_local, groups, HEAD)
        key_rows = rotate(key_f.reshape(all_rows, kv_local, HEAD), heads_position).astype(
            jnp.bfloat16
        )
        value_rows = value_f.astype(jnp.bfloat16).reshape(all_rows, kv_local, HEAD)
        mixed = attend(queries, key_rows, value_rows, heads_program, heads_valid)
        rows_now = lax.dynamic_slice_in_dim(whole, row_first, own_rows, 0)
        summed = lax.psum_scatter(
            jnp.dot(mixed, output_weight[0], preferred_element_type=jnp.float32).astype(
                jnp.bfloat16
            ),
            "tensor",
            scatter_dimension=0,
            tiled=True,
        ).astype(jnp.float32)
        mapped = (rows_now.astype(jnp.float32) + summed).astype(jnp.bfloat16)
        rows_out = jnp.where(active, mapped, rows_now)
        program, position, valid = row_layout(tokens, row_first, own_rows)
        member = (
            (program[None, :] == jnp.arange(prog_count, dtype=jnp.int32)[:, None]) & valid[None, :]
        ).astype(jnp.bfloat16)
        part_list.append(jnp.dot(member, rows_out, preferred_element_type=jnp.float32))
        token_list.append(tokens)
        lists_list.append(lists)
        outgoing = jnp.where(is_last, incoming[tick], rows_out)
        sent_tokens = jnp.where(is_last, incoming_tokens[tick], tokens)
        sent_lists = jnp.where(is_last, jnp.zeros_like(lists), lists)
        whole, tokens, lists = from_behind(
            (assemble(outgoing), sent_tokens, sent_lists), "section", 1
        )
    state_rows = lax.dynamic_slice_in_dim(whole, row_first, own_rows, 0)
    parts = jnp.stack(part_list)
    counts = jnp.stack(token_list)
    exit_lists = jnp.stack(lists_list)
    total = lax.psum(parts.astype(jnp.bfloat16), "tensor").astype(jnp.float32)
    means = total / counts[..., None].astype(jnp.float32)
    embedded = means * lax.rsqrt(jnp.mean(means * means, axis=-1, keepdims=True) + EPS)
    embedded, exit_lists = (
        broadcast(embedded.astype(jnp.bfloat16), "section", section_count - 1).astype(
            embedded.dtype
        ),
        broadcast(as_sent(exit_lists), "section", section_count - 1).astype(exit_lists.dtype),
    )
    flat = embedded.reshape(-1, embedded.shape[-1])
    flat_lists = exit_lists.reshape(-1)
    list_total = list_rows.shape[0]
    target = jnp.sum(
        jnp.where(
            flat_lists[:, None] == jnp.arange(list_total, dtype=jnp.int32)[None, :],
            list_rows[None, :],
            0,
        ),
        axis=1,
    )
    local_count = list_total // (section_count * tensor_count)
    owned = lax.axis_index(("section", "tensor")) * local_count + jnp.arange(
        local_count, dtype=jnp.int32
    )
    select = (owned[:, None] == target[None, :]).astype(jnp.float32)
    list_sums = jnp.dot(select, flat, precision=lax.Precision.HIGHEST)
    return (state_rows[None], list_sums)


def solution(mesh):
    in_specs = (
        P("section", "tensor", None),
        P("section", None),
        P("section", None),
        P(None, "tensor", None),
        P(),
        P("section", None),
        P("section", None, "tensor"),
        P("section", "tensor"),
        P("section", None, "tensor"),
        P("section", "tensor"),
        P("section", None, "tensor"),
        P("section", "tensor"),
        P("section", "tensor", None),
        P(),
    )
    out_specs = (P("section", "tensor", None), P(("section", "tensor"), None))
    return jax.shard_map(local, mesh=mesh, in_specs=in_specs, out_specs=out_specs, check_vma=False)
```

profile of v0, /device:TPU:0, one launch (start us, length us, event | category | flops | bytes accessed | tf_op | source)
XLA Modules:
  0.0 579.1 jit_solution(16477160890725204429)
XLA Ops:
  7.2 0.7 all-gather.9.cloned.1.call-update
  8.0 0.7 broadcast_select_fusion.1
  8.7 0.7 reduce.5
  9.4 0.8 reduce.4
  10.2 0.7 and_select_fusion.2
  10.8 0.2 reduce-window.12
  11.1 0.7 fusion.116
  11.8 0.7 select_reduce_fusion.3
  12.6 0.2 compare_and_fusion.1
  12.8 3.1 collective-permute-done.1
  15.9 0.2 reduce-window.13
  16.3 0.5 copy-done.25
  16.8 2.7 multiply_cosine_fusion
  19.5 36.6 %all-gather.9.cloned.1.call-done = bf16[1,512,3584]{2,1,0:T(8,128)(2,1)} async-done(((bf16[1,128,3584]{2,1,0:T(8,128)(2,1)}), bf16[1,512,3584]{2,1,0:T(8,128)(2,1)}) %all-gather.9.cloned.1.call-update) | async-done | bytes 3670032 | tf_op jit(solution)/shard_map/all_gather | solution.py:118
  56.1 3.0 fusion.3
  59.1 0.1 copy-done.3
  59.2 1.5 fusion.47
  60.7 1.2 fusion.93
  61.9 0.1 copy-done.34
  62.0 5.3 fusion.32
  67.3 2.0 copy.34
  69.3 1.5 fusion.132
  70.8 1.7 copy.57
  72.5 3.0 copy.56
  75.5 2.1 subtract_convert_fusion.1
  77.6 2.1 fusion.22
  79.7 1.6 fusion.6
  81.3 1.4 copy-done.2
  82.6 7.6 %fusion.38 = bf16[128,7,512]{2,0,1:T(8,128)(2,1)S(1)} fusion(f32[7,512]{1,0:T(8,128)S(1)} %fusion.6, f32[7,512]{1,0:T(8,128)S(1)} %get-tuple-element.72, f32[512,512,7]{1,0,2:T(8,128)} %copy-done.2, pred[512,512]{0,1:T(8,128)(4,1)S(1)} %compare_and_fusion.1, bf16[1,3584,128]{2,1,0:T(8,128)(2,1)S(1)} %copy-done, f32[128]{0:T(128)S(1)} %bitcast.180, ...), kind=kOutput, calls=%fused_computation.48 | convolution fusion | flops 956628992 | bytes 13152768 | tf_op jit(solution)/shard_map/while/body/eval_jaxpr/cgqk,kcd->qcgd/dot_general | solution.py:71
  90.2 8.3 %fusion.16 = bf16[512,3584]{1,0:T(8,128)(2,1)} fusion(bf16[512,896]{0,1:T(8,128)(2,1)S(1)} %bitcast.183, bf16[1,896,3584]{2,1,0:T(8,128)(2,1)} %param.26), kind=kOutput, calls=%fused_computation.26 | convolution fusion | flops 3290169344 | bytes 11010048 | tf_op jit(solution)/shard_map/dot_general | solution.py:151
  98.6 42.9 %reduce-scatter.3.cloned.1.call-done = bf16[128,3584]{1,0:T(8,128)(2,1)} async-done(((bf16[512,3584]{1,0:T(8,128)(2,1)}), bf16[128,3584]{1,0:T(8,128)(2,1)}) %reduce-scatter.3.cloned.1.call-update) | async-done | bytes 917520 | tf_op jit(solution)/shard_map/reduce_scatter | solution.py:150
  141.5 2.8 bitcast_select_fusion.2
  144.3 43.7 %all-gather.5.cloned.1.call-done = bf16[512,3584]{1,0:T(8,128)(2,1)} async-done(((bf16[128,3584]{1,0:T(8,128)(2,1)}), bf16[512,3584]{1,0:T(8,128)(2,1)}) %all-gather.5.cloned.1.call-update) | async-done | bytes 3670032 | tf_op jit(solution)/shard_map/all_gather | solution.py:118
  188.1 0.2 collective-permute-start
  188.3 0.2 compare_and_fusion
  188.5 45.6 %collective-permute-done = bf16[512,3584]{1,0:T(8,128)(2,1)S(1)} collective-permute-done((bf16[512,3584]{1,0:T(8,128)(2,1)}, bf16[512,3584]{1,0:T(8,128)(2,1)S(1)}, u32[]{:S(2)}, u32[]{:S(2)}) %collective-permute-start) | collective-permute-done | bytes 3670048 | tf_op jit(solution)/shard_map/ppermute | solution.py:17
  234.1 0.8 fusion
  234.9 2.2 fusion.46
  237.2 1.2 fusion.95
  238.4 8.1 %fusion.35 = f32[512,896]{1,0:T(8,128)} fusion(bf16[1,3584,896]{2,1,0:T(8,128)(2,1)} %param.20, f32[896]{0:T(1024)S(1)} %copy-done.22, bf16[512,3584]{1,0:T(8,128)(2,1)S(1)} %collective-permute-done, f32[512]{0:T(512)S(1)} %add_rsqrt_fusion, f32[3584]{0:T(1024)S(1)} %copy-done.13), kind=kOutput, calls=%fused_computation.47 | convolution fusion | flops 3296133120 | bytes 11947520 | tf_op jit(solution)/shard_map/dot_general | solution.py:130
  246.5 1.8 copy.40
  248.3 1.5 fusion.131
  249.8 1.7 copy.59
  251.5 3.0 copy.58
  254.5 2.0 subtract_convert_fusion
  256.5 2.1 fusion.23
  258.6 3.0 copy-done.1
  261.6 1.6 fusion.7
  263.1 7.6 %fusion.41 = bf16[128,7,512]{2,0,1:T(8,128)(2,1)S(1)} fusion(f32[7,512]{1,0:T(8,128)S(1)} %fusion.7, f32[7,512]{1,0:T(8,128)S(1)} %get-tuple-element.74, f32[512,512,7]{1,0,2:T(8,128)} %copy-done.1, pred[512,512]{0,1:T(8,128)(4,1)S(1)} %compare_and_fusion, bf16[1,3584,128]{2,1,0:T(8,128)(2,1)S(1)} %copy-done, f32[128]{0:T(128)S(1)} %bitcast.181, ...), kind=kOutput, calls=%fused_computation.49 | convolution fusion | flops 956628992 | bytes 13152768 | tf_op jit(solution)/shard_map/while/body/eval_jaxpr/cgqk,kcd->qcgd/dot_general | solution.py:71
  270.7 8.3 %fusion.19 = bf16[512,3584]{1,0:T(8,128)(2,1)} fusion(bf16[512,896]{0,1:T(8,128)(2,1)S(1)} %bitcast.182, bf16[1,896,3584]{2,1,0:T(8,128)(2,1)} %param.26), kind=kOutput, calls=%fused_computation.27 | convolution fusion | flops 3290169344 | bytes 11010048 | tf_op jit(solution)/shard_map/dot_general | solution.py:151
  279.1 39.6 %reduce-scatter.5.cloned.1.call-done = bf16[128,3584]{1,0:T(8,128)(2,1)} async-done(((bf16[512,3584]{1,0:T(8,128)(2,1)}), bf16[128,3584]{1,0:T(8,128)(2,1)}) %reduce-scatter.5.cloned.1.call-update) | async-done | bytes 917520 | tf_op jit(solution)/shard_map/reduce_scatter | solution.py:150
  318.7 2.8 bitcast_select_fusion.3
  321.5 43.8 %all-gather.7.cloned.1.call-done = bf16[512,3584]{1,0:T(8,128)(2,1)} async-done(((bf16[128,3584]{1,0:T(8,128)(2,1)}), bf16[512,3584]{1,0:T(8,128)(2,1)}) %all-gather.7.cloned.1.call-update) | async-done | bytes 3670032 | tf_op jit(solution)/shard_map/all_gather | solution.py:118
  365.3 1.6 collective-permute-start.3
  366.9 44.3 %collective-permute-done.3 = s32[3]{0:T(128)S(1)} collective-permute-done((s32[3]{0:T(128)S(1)}, s32[3]{0:T(128)S(1)}, u32[]{:S(2)}, u32[]{:S(2)}) %collective-permute-start.3) | collective-permute-done | bytes 44 | tf_op jit(solution)/shard_map/ppermute | solution.py:17
  411.3 13.5 %psum.21 = s32[6]{0:T(128)S(1)} all-reduce(s32[6]{0:T(128)S(1)} %eq.173), channel_id=1, replica_groups=mesh['section'=32,'tensor'=4] {'section'}, use_global_device_ids=true, to_apply=%region_16.17 | all-reduce | flops 6 | bytes 48 | tf_op jit(solution)/shard_map/psum | solution.py:22
  424.9 0.2 select_reduce_fusion
  425.3 1.9 fusion.24
  427.2 1.8 fusion.25
  429.1 15.9 %psum.22 = bf16[2,3,3584]{2,1,0:T(4,128)(2,1)S(1)} all-reduce(bf16[2,3,3584]{2,1,0:T(4,128)(2,1)S(1)} %pad_maximum_fusion), channel_id=1, replica_groups=mesh['section'=32,'tensor'=4] {'tensor'}, use_global_device_ids=true, to_apply=%region_24.25 | all-reduce | flops 21504 | bytes 86016 | tf_op jit(solution)/shard_map/psum | solution.py:177
  445.0 0.2 multiply_reduce_fusion
  445.3 123.9 %psum.23 = bf16[6,3584]{1,0:T(8,128)(2,1)S(1)} all-reduce(bf16[6,3584]{1,0:T(8,128)(2,1)S(1)} %reshape.609), channel_id=1, replica_groups=mesh['section'=32,'tensor'=4] {'section'}, use_global_device_ids=true, to_apply=%region_26.27 | all-reduce | flops 21504 | bytes 86016 | tf_op jit(solution)/shard_map/psum | solution.py:22
  569.2 0.8 fusion.97
  570.0 2.2 dynamic-slice_bitcast_fusion
  (115 shorter events, 1.4 us)
Async XLA Ops:
  7.2 75.5 %copy-start = (bf16[1,3584,128]{2,1,0:T(8,128)(2,1)S(1)}, bf16[1,3584,128]{2,1,0:T(8,128)(2,1)}, u32[]{:S(2)}) copy-start(bf16[1,3584,128]{2,1,0:T(8,128)(2,1)} %param.24) | copy-start | bytes 2752516
  7.2 51.9 %copy-start.35 = (bf16[1,3584,128]{2,1,0:T(8,128)(2,1)S(1)}, bf16[1,3584,128]{2,1,0:T(8,128)(2,1)}, u32[]{:S(2)}) copy-start(bf16[1,3584,128]{2,1,0:T(8,128)(2,1)} %param.22) | copy-start | bytes 2752516
  7.2 51.9 %copy-start.37 = (f32[1,128]{1,0:T(1,128)S(1)}, f32[1,128]{1,0:T(1,128)}, u32[]{:S(2)}) copy-start(f32[1,128]{1,0:T(1,128)} %param.23) | copy-start | bytes 1540
  7.2 48.9 %all-gather.9.cloned.1.call-start = ((), (), s32[]{:S(2)}) async-start(), calls=%async_computation.6 | async-start | bytes 4587520 | tf_op jit(solution)/shard_map/all_gather | solution.py:118
  7.9 133.5 %reduce-scatter.3.cloned.1.call-start = ((), (), s32[]{:S(2)}) async-start(), calls=%async_computation.2 | async-start | bytes 4587520 | tf_op jit(solution)/shard_map/reduce_scatter | solution.py:150
  8.7 7.2 %collective-permute-start.1 = (s32[3]{0:T(128)S(1)}, s32[3]{0:T(128)S(1)}, u32[]{:S(2)}, u32[]{:S(2)}) collective-permute-start(s32[3]{0:T(128)S(1)} %broadcast_select_fusion.1), channel_id=1, source_target_pairs={{124,0},{0,4},{4,8},{8,12},{12,16},{16,20},{20,24},{24,28},{28,32}... | collective-permute-start | bytes 44 | tf_op jit(solution)/shard_map/ppermute | solution.py:17
  9.4 52.5 %copy-start.21 = (f32[896]{0:T(1024)}, f32[896]{0:T(1024)S(1)}, u32[]{:S(2)}) copy-start(f32[896]{0:T(1024)S(1)} %reduce.5) | copy-start | bytes 10756
  10.1 51.8 %copy-start.11 = (f32[3584]{0:T(1024)}, f32[3584]{0:T(1024)S(1)}, u32[]{:S(2)}) copy-start(f32[3584]{0:T(1024)S(1)} %reduce.4) | copy-start | bytes 43012
  11.0 49.7 %copy-start.16 = (f32[64]{0:T(128)}, f32[64]{0:T(128)S(1)}, u32[]{:S(2)}) copy-start(f32[64]{0:T(128)S(1)} %multiply_power_fusion) | copy-start | bytes 772
  11.0 0.8 copy-start.27
  11.8 0.8 copy-start.23
  15.9 3.6 copy-start.18
  16.1 0.7 copy-start.29
  16.2 0.6 copy-start.25
  56.1 3.1 copy-start.3
  59.1 2.8 copy-start.31
  59.2 2.8 copy-start.34
  75.5 2.1 copy-start.9
  75.5 2.1 copy-start.10
  79.7 3.0 copy-start.2
  79.7 3.0 copy-start.12
  79.7 3.0 copy-start.32
  79.7 3.0 copy-start.38
  98.5 43.0 %copy-start.5 = (bf16[2,128,3584]{2,1,0:T(8,128)(2,1)S(1)}, bf16[2,128,3584]{2,1,0:T(8,128)(2,1)}, u32[]{:S(2)}) copy-start(bf16[2,128,3584]{2,1,0:T(8,128)(2,1)} %param.17) | copy-start | bytes 5505028
  98.5 89.5 %all-gather.5.cloned.1.call-start = ((), (), s32[]{:S(2)}) async-start(), calls=%async_computation.3 | async-start | bytes 4587520 | tf_op jit(solution)/shard_map/all_gather | solution.py:118
  144.3 90.6 %copy-start.36 = (bf16[1,3584,128]{2,1,0:T(8,128)(2,1)S(1)}, bf16[1,3584,128]{2,1,0:T(8,128)(2,1)}, u32[]{:S(2)}) copy-start(bf16[1,3584,128]{2,1,0:T(8,128)(2,1)} %param.22) | copy-start | bytes 2752516
  144.3 174.4 %reduce-scatter.5.cloned.1.call-start = ((), (), s32[]{:S(2)}) async-start(), calls=%async_computation.4 | async-start | bytes 4587520 | tf_op jit(solution)/shard_map/reduce_scatter | solution.py:150
  188.1 46.0 %collective-permute-start = (bf16[512,3584]{1,0:T(8,128)(2,1)}, bf16[512,3584]{1,0:T(8,128)(2,1)S(1)}, u32[]{:S(2)}, u32[]{:S(2)}) collective-permute-start(bf16[512,3584]{1,0:T(8,128)(2,1)} %all-gather.5.cloned.1.call-done), channel_id=1, source_target_pairs={{124,0},{0,4},{4,8},{8,12},{12,16},{16,20},{20,24},{24,28},{28,32}... | collective-permute-start | bytes 11010056 | tf_op jit(solution)/shard_map/ppermute | solution.py:17
  234.1 4.3 copy-start.4
  234.9 2.3 copy-start.17
  234.9 3.5 copy-start.13
  234.9 3.5 copy-start.22
  254.5 2.0 copy-start.7
  254.5 2.0 copy-start.8
  258.6 3.0 copy-start.1
  261.6 1.6 copy-start.14
  261.6 1.6 copy-start.39
  279.0 39.7 %copy-start.6 = (bf16[2,128,3584]{2,1,0:T(8,128)(2,1)S(1)}, bf16[2,128,3584]{2,1,0:T(8,128)(2,1)}, u32[]{:S(2)}) copy-start(bf16[2,128,3584]{2,1,0:T(8,128)(2,1)} %param.17) | copy-start | bytes 5505028
  279.0 86.3 %copy-start.33 = (s32[1,3]{1,0:T(1,128)S(1)}, s32[1,3]{1,0:T(1,128)}, u32[]{:S(2)}) copy-start(s32[1,3]{1,0:T(1,128)} %param.16) | copy-start | bytes 40
  279.0 145.8 %copy-start.15 = (s32[1,3]{1,0:T(1,128)S(1)}, s32[1,3]{1,0:T(1,128)}, u32[]{:S(2)}) copy-start(s32[1,3]{1,0:T(1,128)} %param.15) | copy-start | bytes 40
  279.0 145.8 %copy-start.19 = (s32[3]{0:T(128)S(1)}, s32[3]{0:T(128)}, u32[]{:S(2)}) copy-start(s32[3]{0:T(128)} %copy-done.18) | copy-start | bytes 40
  279.0 145.8 %copy-start.20 = (s32[1024]{0:T(1024)S(1)}, s32[1024]{0:T(1024)}, u32[]{:S(2)}) copy-start(s32[1024]{0:T(1024)} %param.27) | copy-start | bytes 12292
  279.0 146.0 %copy-start.28 = (s32[3]{0:T(128)S(1)}, s32[3]{0:T(128)}, u32[]{:S(2)}) copy-start(s32[3]{0:T(128)} %copy-done.27) | copy-start | bytes 40
  279.0 146.0 %copy-start.30 = (s32[3]{0:T(128)S(1)}, s32[3]{0:T(128)}, u32[]{:S(2)}) copy-start(s32[3]{0:T(128)} %copy-done.29) | copy-start | bytes 40
  279.1 146.1 %copy-start.24 = (s32[3]{0:T(128)S(1)}, s32[3]{0:T(128)}, u32[]{:S(2)}) copy-start(s32[3]{0:T(128)} %copy-done.23) | copy-start | bytes 40
  279.1 146.2 %copy-start.26 = (s32[3]{0:T(128)S(1)}, s32[3]{0:T(128)}, u32[]{:S(2)}) copy-start(s32[3]{0:T(128)} %copy-done.25) | copy-start | bytes 40
  279.1 86.2 %all-gather.7.cloned.1.call-start = ((), (), s32[]{:S(2)}) async-start(), calls=%async_computation.5 | async-start | bytes 4587520 | tf_op jit(solution)/shard_map/all_gather | solution.py:118
  365.3 204.8 %collective-permute-start.2 = (bf16[512,3584]{1,0:T(8,128)(2,1)}, bf16[512,3584]{1,0:T(8,128)(2,1)}, u32[]{:S(2)}, u32[]{:S(2)}) collective-permute-start(bf16[512,3584]{1,0:T(8,128)(2,1)} %all-gather.7.cloned.1.call-done), channel_id=1, source_target_pairs={{124,0},{0,4},{4,8},{8,12},{12,16},{16,20},{20,24},{24,28},{28,32}... | collective-permute-start | bytes 11010056 | tf_op jit(solution)/shard_map/ppermute | solution.py:17
  365.3 45.9 %collective-permute-start.3 = (s32[3]{0:T(128)S(1)}, s32[3]{0:T(128)S(1)}, u32[]{:S(2)}, u32[]{:S(2)}) collective-permute-start(s32[3]{0:T(128)S(1)} %fusion.115), channel_id=1, source_target_pairs={{124,0},{0,4},{4,8},{8,12},{12,16},{16,20},{20,24},{24,28},{28,32}... | collective-permute-start | bytes 44 | tf_op jit(solution)/shard_map/ppermute | solution.py:17
Sparse Core Ops, SparseCore 0:
  9.7 46.3 all-gather.8
  98.7 42.7 reduce-scatter.2
  144.4 43.6 all-gather.4
  279.2 39.4 reduce-scatter.4
  321.6 43.6 all-gather.6
where the time goes:
time: 586 us; the launch traced here: 579 us
  waiting for transfers between devices  300 us (51%)
  blocking collectives  153 us (26%)
  matrix products  57.4 us (10%)
  other arithmetic  27.9 us (5%)
  local copies, waits for them, and re-layouts  23.6 us (4%)
  between operations  14.7 us (3%)
    psum x2, blocking collectives, broadcast(): return lax.psum(jnp.where(mine, value, jnp.zeros_like(value)), axis)  137 us
    all_gather x3, waiting for transfers between devices, assemble(): return lax.all_gather(rows, 'tensor', axis=0, tiled=True)  124 us
    ppermute x4, waiting for transfers between devices, from_behind(): return lax.ppermute(block, axis, route)  93 us
    reduce_scatter x2, waiting for transfers between devices, local(): lax.psum_scatter(jnp.dot(mixed, output_weight[0], preferred_element_type=...  82.4 us
    dot_general x2, matrix products, local(): jnp.dot(mixed, output_weight[0], preferred_element_type=jnp.float32)  16.6 us
    psum x1, blocking collectives, local(): total = lax.psum(parts.astype(jnp.bfloat16), 'tensor').astype(jnp.float32)  15.9 us
    dot_general x2, matrix products, one_block(): jnp.einsum('cgqk,kcd->qcgd', probs, value_rows, preferred_element_type=jn...  15.2 us
    unnamed x84, local copies, waits for them, and re-layouts  14.6 us
  transfers between devices with their start and end apart: 9, of which 8 were waited for; matrix products, arithmetic and copies ran while one was open for 2% of the time, Pallas kernels for 0%

commit v1 on v0

--- a/solution.py
+++ b/solution.py
@@ -9,6 +9,19 @@
 BLOCK = 128
 EPS = 1e-06
 THETA = 1000000.0
+
+
+def collect(x, axis, dim):
+    ways = lax.axis_size(axis)
+    up = [(d, (d + 1) % ways) for d in range(ways)]
+    down = [(d, (d - 1) % ways) for d in range(ways)]
+    earlier, later = ([x], [x])
+    for _ in range(ways // 2):
+        earlier.append(lax.ppermute(earlier[-1], axis, up))
+    for _ in range((ways - 1) // 2):
+        later.append(lax.ppermute(later[-1], axis, down))
+    line = jnp.concatenate([*earlier[::-1], *later[1:]], axis=dim)
+    return jnp.roll(line, (lax.axis_index(axis) - ways // 2) * x.shape[dim], axis=dim)
 
 
 def from_behind(block, axis, distance):
@@ -115,7 +128,7 @@
     prog_count = flight_tokens.shape[1]
 
     def assemble(rows):
-        return lax.all_gather(rows, "tensor", axis=0, tiled=True)
+        return collect(rows, "tensor", 0)
 
     tokens = flight_tokens[0]
     lists = flight_lists[0]

time: 586 us -> 619 us (1.056)
  other arithmetic: 27.9 us -> 58.5 us
  waiting for transfers between devices: 300 us -> 290 us
  starting transfers between devices: 2 us -> 11.9 us
    all_gather x3 -> x0, waiting for transfers between devices: 124 us -> none  [assemble(): return lax.all_gather(rows, 'tensor', axis=0, tiled=True)]
    ppermute x0 -> x9, waiting for transfers between devices: none -> 119 us  [the longest x6 119 us: collect(): earlier.append(lax.ppermute(earlier[-1], axis, up))]
    concatenate x0 -> x3, other arithmetic: none -> 31.6 us  [collect(): jnp.roll(line, (lax.axis_index(axis) - ways // 2) * x.shape[dim], axis=dim)]
    ppermute x0 -> x9, starting transfers between devices: none -> 10.1 us  [the longest x3 8.88 us: collect(): later.append(lax.ppermute(later[-1], axis, down))]
    unnamed x84 -> x90, local copies, waits for them, and re-layouts: 14.6 us -> 16.2 us
  transfers between devices with their start and end apart: 9 -> 15, of which waited for: 8 -> 11; matrix products, arithmetic and copies ran while one was open for 2% -> 3% of each run, Pallas kernels for 0% -> 0%
where the time goes in v1:
time: 619 us; the launch traced here: 612 us
  waiting for transfers between devices  290 us (47%)
  blocking collectives  152 us (25%)
  matrix products  59 us (10%)
  other arithmetic  58.5 us (9%)
  local copies, waits for them, and re-layouts  25.3 us (4%)
  between operations  14.9 us (2%)
  starting transfers between devices  11.9 us (2%)
    psum x2, blocking collectives, broadcast(): return lax.psum(jnp.where(mine, value, jnp.zeros_like(value)), axis)  137 us
    ppermute x6, waiting for transfers between devices, collect(): earlier.append(lax.ppermute(earlier[-1], axis, up))  119 us
    ppermute x4, waiting for transfers between devices, from_behind(): return lax.ppermute(block, axis, route)  90.3 us
    reduce_scatter x2, waiting for transfers between devices, local(): lax.psum_scatter(jnp.dot(mixed, output_weight[0], preferred_element_type=...  80.7 us
    concatenate x3, other arithmetic, collect(): jnp.roll(line, (lax.axis_index(axis) - ways // 2) * x.shape[dim], axis=dim)  31.6 us
    dot_general x2, matrix products, local(): jnp.dot(mixed, output_weight[0], preferred_element_type=jnp.float32)  18.3 us
    dot_general x2, matrix products, one_block(): jnp.einsum('cgqk,kcd->qcgd', probs, value_rows, preferred_element_type=jn...  17 us
    unnamed x90, local copies, waits for them, and re-layouts  16.2 us
  transfers between devices with their start and end apart: 15, of which 11 were waited for; matrix products, arithmetic and copies ran while one was open for 3% of the time, Pallas kernels for 0%

profile of v1, /device:TPU:0, one launch (start us, length us, event | category | flops | bytes accessed | tf_op | source)
XLA Modules:
  0.0 611.7 jit_solution(16859063835080431067)
XLA Ops:
  7.2 2.9 collective-permute-start.2
  10.1 0.7 broadcast_select_fusion.1
  10.8 0.7 and_select_fusion.2
  11.7 0.7 fusion.130
  12.9 0.7 select_reduce_fusion.3
  14.2 1.3 reduce.5
  15.4 1.3 reduce.4
  17.1 0.6 collective-permute-done.7
  17.9 15.5 %collective-permute-done = bf16[128,3584]{1,0:T(8,128)(2,1)S(1)} collective-permute-done((bf16[128,3584]{1,0:T(8,128)(2,1)}, bf16[128,3584]{1,0:T(8,128)(2,1)S(1)}, u32[]{:S(2)}, u32[]{:S(2)}) %collective-permute-start) | collective-permute-done | bytes 917536 | tf_op jit(solution)/shard_map/ppermute | solution.py:20
  33.5 0.7 select_reduce_fusion.1
  34.2 3.3 multiply_cosine_fusion
  37.5 18.0 %collective-permute-done.1 = bf16[128,3584]{1,0:T(8,128)(2,1)S(1)} collective-permute-done((bf16[128,3584]{1,0:T(8,128)(2,1)S(1)}, bf16[128,3584]{1,0:T(8,128)(2,1)S(1)}, u32[]{:S(2)}, u32[]{:S(2)}) %collective-permute-start.1) | collective-permute-done | bytes 917536 | tf_op jit(solution)/shard_map/ppermute | solution.py:20
  55.5 3.1 maximum_maximum_fusion
  58.6 0.8 fusion
  59.4 1.5 fusion.61
  60.9 1.2 fusion.107
  62.2 5.4 fusion.46
  67.6 2.0 copy.34
  69.6 1.5 fusion.146
  71.1 1.7 copy.57
  72.8 3.1 copy.56
  75.8 2.1 subtract_convert_fusion.1
  77.9 2.9 fusion.22
  80.9 3.0 copy-done.2
  83.9 1.6 fusion.6
  85.5 8.5 %fusion.52 = bf16[128,7,512]{2,0,1:T(8,128)(2,1)} fusion(f32[7,512]{1,0:T(8,128)S(1)} %fusion.6, f32[7,512]{1,0:T(8,128)S(1)} %get-tuple-element.73, f32[512,512,7]{1,0,2:T(8,128)} %copy-done.2, pred[512,512]{0,1:T(8,128)(4,1)S(1)} %compare_and_fusion.1, bf16[1,3584,128]{2,1,0:T(8,128)(2,1)S(1)} %copy-done, f32[128]{0:T(128)S(1)} %bitcast.175, ...), kind=kOutput, calls=%fused_computation.79 | convolution fusion | flops 956628992 | bytes 13152772 | tf_op jit(solution)/shard_map/while/body/eval_jaxpr/cgqk,kcd->qcgd/dot_general | solution.py:84
  94.0 9.1 %fusion.16 = bf16[512,3584]{1,0:T(8,128)(2,1)} fusion(bf16[512,896]{0,1:T(8,128)(2,1)} %bitcast.178, bf16[1,896,3584]{2,1,0:T(8,128)(2,1)} %param.28), kind=kOutput, calls=%fused_computation.43 | convolution fusion | flops 3290169344 | bytes 11010048 | tf_op jit(solution)/shard_map/dot_general | solution.py:164
  103.3 42.5 %reduce-scatter.3.cloned.1.call-done = bf16[128,3584]{1,0:T(8,128)(2,1)} async-done(((bf16[512,3584]{1,0:T(8,128)(2,1)}), bf16[128,3584]{1,0:T(8,128)(2,1)}) %reduce-scatter.3.cloned.1.call-update) | async-done | bytes 917520 | tf_op jit(solution)/shard_map/reduce_scatter | solution.py:163
  145.8 2.1 bitcast_select_fusion.2
  147.8 0.7 collective-permute-start.3
  148.6 3.0 collective-permute-start.5
  151.6 20.1 %collective-permute-done.3 = bf16[128,3584]{1,0:T(8,128)(2,1)S(1)} collective-permute-done((bf16[128,3584]{1,0:T(8,128)(2,1)S(1)}, bf16[128,3584]{1,0:T(8,128)(2,1)S(1)}, u32[]{:S(2)}, u32[]{:S(2)}) %collective-permute-start.3) | collective-permute-done | bytes 917536 | tf_op jit(solution)/shard_map/ppermute | solution.py:20
  171.7 22.5 %collective-permute-done.4 = bf16[128,3584]{1,0:T(8,128)(2,1)S(1)} collective-permute-done((bf16[128,3584]{1,0:T(8,128)(2,1)S(1)}, bf16[128,3584]{1,0:T(8,128)(2,1)S(1)}, u32[]{:S(2)}, u32[]{:S(2)}) %collective-permute-start.4) | collective-permute-done | bytes 917536 | tf_op jit(solution)/shard_map/ppermute | solution.py:20
  194.1 15.4 %fusion.36 = bf16[512,3584]{1,0:T(8,128)(2,1)S(1)} fusion(s32[]{:T(128)S(6)} %select_n.164, bf16[128,3584]{1,0:T(8,128)(2,1)S(1)} %collective-permute-done.4, bf16[128,3584]{1,0:T(8,128)(2,1)S(1)} %collective-permute-done.3, bf16[128,3584]{1,0:T(8,128)(2,1)S(1)} %bitcast_select_fusion.2, bf16[128,3584]{1,0:T(8,128)(2,1)S(1)} %collective-permute-done.5), kind=kLoop, calls=%fused_computation.61 | loop fusion | flops 29360128 | bytes 7340036 | tf_op jit(solution)/shard_map/jit(_roll_dynamic)/concatenate | solution.py:24
  209.9 45.3 %collective-permute-done.6 = bf16[512,3584]{1,0:T(8,128)(2,1)S(1)} collective-permute-done((bf16[512,3584]{1,0:T(8,128)(2,1)S(1)}, bf16[512,3584]{1,0:T(8,128)(2,1)S(1)}, u32[]{:S(2)}, u32[]{:S(2)}) %collective-permute-start.6) | collective-permute-done | bytes 3670048 | tf_op jit(solution)/shard_map/ppermute | solution.py:30
  255.3 0.8 fusion.3
  256.1 1.5 fusion.60
  257.6 1.2 fusion.109
  258.8 5.4 fusion.49
  264.2 2.0 copy.40
  266.2 1.5 fusion.145
  267.6 1.7 copy.59
  269.4 3.1 copy.58
  272.4 2.0 subtract_convert_fusion
  274.4 2.9 fusion.23
  277.4 3.0 copy-done.1
  280.4 1.6 fusion.7
  282.0 8.5 %fusion.55 = bf16[128,7,512]{2,0,1:T(8,128)(2,1)} fusion(f32[7,512]{1,0:T(8,128)S(1)} %fusion.7, f32[7,512]{1,0:T(8,128)S(1)} %get-tuple-element.75, f32[512,512,7]{1,0,2:T(8,128)} %copy-done.1, pred[512,512]{0,1:T(8,128)(4,1)S(1)} %compare_and_fusion, bf16[1,3584,128]{2,1,0:T(8,128)(2,1)S(1)} %copy-done, f32[128]{0:T(128)S(1)} %bitcast.176, ...), kind=kOutput, calls=%fused_computation.80 | convolution fusion | flops 956628992 | bytes 13152768 | tf_op jit(solution)/shard_map/while/body/eval_jaxpr/cgqk,kcd->qcgd/dot_general | solution.py:84
  290.5 9.1 %fusion.19 = bf16[512,3584]{1,0:T(8,128)(2,1)} fusion(bf16[512,896]{0,1:T(8,128)(2,1)} %bitcast.177, bf16[1,896,3584]{2,1,0:T(8,128)(2,1)} %param.28), kind=kOutput, calls=%fused_computation.44 | convolution fusion | flops 3290169344 | bytes 11010048 | tf_op jit(solution)/shard_map/dot_general | solution.py:164
  299.7 38.2 %reduce-scatter.5.cloned.1.call-done = bf16[128,3584]{1,0:T(8,128)(2,1)} async-done(((bf16[512,3584]{1,0:T(8,128)(2,1)}), bf16[128,3584]{1,0:T(8,128)(2,1)}) %reduce-scatter.5.cloned.1.call-update) | async-done | bytes 917520 | tf_op jit(solution)/shard_map/reduce_scatter | solution.py:163
  337.9 1.8 bitcast_select_fusion.3
  340.3 3.0 collective-permute-start.10
  343.3 20.1 %collective-permute-done.8 = bf16[128,3584]{1,0:T(8,128)(2,1)S(1)} collective-permute-done((bf16[128,3584]{1,0:T(8,128)(2,1)S(1)}, bf16[128,3584]{1,0:T(8,128)(2,1)S(1)}, u32[]{:S(2)}, u32[]{:S(2)}) %collective-permute-start.8) | collective-permute-done | bytes 917536 | tf_op jit(solution)/shard_map/ppermute | solution.py:20
  363.5 22.5 %collective-permute-done.9 = bf16[128,3584]{1,0:T(8,128)(2,1)S(1)} collective-permute-done((bf16[128,3584]{1,0:T(8,128)(2,1)S(1)}, bf16[128,3584]{1,0:T(8,128)(2,1)S(1)}, u32[]{:S(2)}, u32[]{:S(2)}) %collective-permute-start.9) | collective-permute-done | bytes 917536 | tf_op jit(solution)/shard_map/ppermute | solution.py:20
  386.0 13.2 %fusion.29 = bf16[512,3584]{1,0:T(8,128)(2,1)} fusion(s32[]{:T(128)S(6)} %select_n.164, bf16[128,3584]{1,0:T(8,128)(2,1)S(1)} %collective-permute-done.9, bf16[128,3584]{1,0:T(8,128)(2,1)S(1)} %collective-permute-done.8, bf16[128,3584]{1,0:T(8,128)(2,1)S(1)} %bitcast_select_fusion.3, bf16[128,3584]{1,0:T(8,128)(2,1)S(1)} %collective-permute-done.10), kind=kLoop, calls=%fused_computation.54 | loop fusion | flops 29360128 | bytes 7340036 | tf_op jit(solution)/shard_map/jit(_roll_dynamic)/concatenate | solution.py:24
  399.1 1.6 collective-permute-start.12
  400.7 44.3 %collective-permute-done.12 = s32[3]{0:T(128)S(1)} collective-permute-done((s32[3]{0:T(128)S(1)}, s32[3]{0:T(128)S(1)}, u32[]{:S(2)}, u32[]{:S(2)}) %collective-permute-start.12) | collective-permute-done | bytes 44 | tf_op jit(solution)/shard_map/ppermute | solution.py:30
  445.2 13.5 %psum.21 = s32[6]{0:T(128)S(1)} all-reduce(s32[6]{0:T(128)S(1)} %eq.175), channel_id=1, replica_groups=mesh['section'=32,'tensor'=4] {'section'}, use_global_device_ids=true, to_apply=%region_16.18 | all-reduce | flops 6 | bytes 48 | tf_op jit(solution)/shard_map/psum | solution.py:35
  459.2 1.7 fusion.24
  460.9 1.6 fusion.25
  462.5 14.9 %psum.22 = bf16[2,3,3584]{2,1,0:T(4,128)(2,1)S(1)} all-reduce(bf16[2,3,3584]{2,1,0:T(4,128)(2,1)S(1)} %pad_maximum_fusion), channel_id=1, replica_groups=mesh['section'=32,'tensor'=4] {'tensor'}, use_global_device_ids=true, to_apply=%region_24.26 | all-reduce | flops 21504 | bytes 86016 | tf_op jit(solution)/shard_map/psum | solution.py:190
  477.8 123.9 %psum.23 = bf16[6,3584]{1,0:T(8,128)(2,1)S(1)} all-reduce(bf16[6,3584]{1,0:T(8,128)(2,1)S(1)} %reshape.609), channel_id=1, replica_groups=mesh['section'=32,'tensor'=4] {'section'}, use_global_device_ids=true, to_apply=%region_26.28 | all-reduce | flops 21504 | bytes 86016 | tf_op jit(solution)/shard_map/psum | solution.py:35
  601.6 0.8 fusion.113
  602.5 2.2 dynamic-slice_bitcast_fusion
  (135 shorter events, 4.0 us)
Async XLA Ops:
  7.2 78.3 %copy-start = (bf16[1,3584,128]{2,1,0:T(8,128)(2,1)S(1)}, bf16[1,3584,128]{2,1,0:T(8,128)(2,1)}, u32[]{:S(2)}) copy-start(bf16[1,3584,128]{2,1,0:T(8,128)(2,1)} %param.26) | copy-start | bytes 2752516
  7.2 138.6 %reduce-scatter.3.cloned.1.call-start = ((), (), s32[]{:S(2)}) async-start(), calls=%async_computation.2 | async-start | bytes 4587520 | tf_op jit(solution)/shard_map/reduce_scatter | solution.py:163
  7.2 30.2 %collective-permute-start.2 = (bf16[128,3584]{1,0:T(8,128)(2,1)}, bf16[128,3584]{1,0:T(8,128)(2,1)S(1)}, u32[]{:S(2)}, u32[]{:S(2)}) collective-permute-start(bf16[128,3584]{1,0:T(8,128)(2,1)} %bitcast.162), channel_id=1, source_target_pairs={{0,3},{1,0},{2,1},{3,2},{4,7},{5,4},{6,5},{7,6},{8,11},{9,8},{10,9... | collective-permute-start | bytes 2752520 | tf_op jit(solution)/shard_map/ppermute | solution.py:22
  10.1 23.2 %collective-permute-start = (bf16[128,3584]{1,0:T(8,128)(2,1)}, bf16[128,3584]{1,0:T(8,128)(2,1)S(1)}, u32[]{:S(2)}, u32[]{:S(2)}) collective-permute-start(bf16[128,3584]{1,0:T(8,128)(2,1)} %bitcast.163), channel_id=1, source_target_pairs={{0,1},{1,2},{2,3},{3,0},{4,5},{5,6},{6,7},{7,4},{8,9},{9,10},{10,1... | collective-permute-start | bytes 2752520 | tf_op jit(solution)/shard_map/ppermute | solution.py:20
  10.8 6.9 %collective-permute-start.7 = (s32[3]{0:T(128)S(1)}, s32[3]{0:T(128)S(1)}, u32[]{:S(2)}, u32[]{:S(2)}) collective-permute-start(s32[3]{0:T(128)S(1)} %broadcast_select_fusion.1), channel_id=1, source_target_pairs={{124,0},{0,4},{4,8},{8,12},{12,16},{16,20},{20,24},{24,28},{28,32}... | collective-permute-start | bytes 44 | tf_op jit(solution)/shard_map/ppermute | solution.py:30
  12.3 4.5 copy-start.22
  12.4 0.5 copy-start.26
  17.7 16.5 %copy-start.17 = (s32[3]{0:T(128)}, s32[3]{0:T(128)S(1)}, u32[]{:S(2)}) copy-start(s32[3]{0:T(128)S(1)} %collective-permute-done.7) | copy-start | bytes 40
  17.9 15.5 %copy-start.28 = (s32[3]{0:T(128)}, s32[3]{0:T(128)S(1)}, u32[]{:S(2)}) copy-start(s32[3]{0:T(128)S(1)} %multiply_bitcast_fusion) | copy-start | bytes 40
  33.4 22.1 %collective-permute-start.1 = (bf16[128,3584]{1,0:T(8,128)(2,1)S(1)}, bf16[128,3584]{1,0:T(8,128)(2,1)S(1)}, u32[]{:S(2)}, u32[]{:S(2)}) collective-permute-start(bf16[128,3584]{1,0:T(8,128)(2,1)S(1)} %collective-permute-done), channel_id=1, source_target_pairs={{0,1},{1,2},{2,3},{3,0},{4,5},{5,6},{6,7},{7,4},{8,9},{9,10},{10,1... | collective-permute-start | bytes 2752520 | tf_op jit(solution)/shard_map/ppermute | solution.py:20
  33.5 0.7 copy-start.24
  37.5 21.9 %copy-start.9 = (f32[3584]{0:T(1024)S(1)}, f32[3584]{0:T(1024)}, u32[]{:S(2)}) copy-start(f32[3584]{0:T(1024)} %reduce.4) | copy-start | bytes 43012
  37.5 22.0 %copy-start.33 = (bf16[1,3584,128]{2,1,0:T(8,128)(2,1)S(1)}, bf16[1,3584,128]{2,1,0:T(8,128)(2,1)}, u32[]{:S(2)}) copy-start(bf16[1,3584,128]{2,1,0:T(8,128)(2,1)} %param.24) | copy-start | bytes 2752516
  37.5 22.0 %copy-start.35 = (f32[1,128]{1,0:T(1,128)S(1)}, f32[1,128]{1,0:T(1,128)}, u32[]{:S(2)}) copy-start(f32[1,128]{1,0:T(1,128)} %param.25) | copy-start | bytes 1540
  55.5 6.7 %slice-start = ((s8[6422528]{0:T(1024)(128)(4,1)}), s8[4194304]{0:T(1024)(128)(4,1)S(1)}, s32[]{:S(2)}) async-start(s8[6422528]{0:T(1024)(128)(4,1)} %bitcast.169), calls=%async_computation.4 | async-start | bytes 8388608
  58.5 3.6 copy-start.3
  58.6 2.4 copy-start.15
  58.6 3.6 copy-start.20
  58.6 3.6 slice-start.1
  59.4 2.8 copy-start.30
  77.9 7.6 %copy-start.10 = (f32[3584]{0:T(1024)S(1)}, f32[3584]{0:T(1024)}, u32[]{:S(2)}) copy-start(f32[3584]{0:T(1024)} %reduce.4) | copy-start | bytes 43012
  77.9 7.6 %copy-start.31 = (f32[512]{0:T(512)S(1)}, f32[512]{0:T(512)}, u32[]{:S(2)}) copy-start(f32[512]{0:T(512)} %copy-done.30) | copy-start | bytes 6148
  77.9 7.6 %copy-start.37 = (f32[1,128]{1,0:T(1,128)S(1)}, f32[1,128]{1,0:T(1,128)}, u32[]{:S(2)}) copy-start(f32[1,128]{1,0:T(1,128)} %param.27) | copy-start | bytes 1540
  80.9 3.0 copy-start.2
  94.0 51.7 %copy-start.5 = (bf16[2,128,3584]{2,1,0:T(8,128)(2,1)S(1)}, bf16[2,128,3584]{2,1,0:T(8,128)(2,1)}, u32[]{:S(2)}) copy-start(bf16[2,128,3584]{2,1,0:T(8,128)(2,1)} %param.19) | copy-start | bytes 5505028
  103.2 106.5 %copy-start.14 = (s32[512]{0:T(512)S(1)}, s32[512]{0:T(512)}, u32[]{:S(2)}) copy-start(s32[512]{0:T(512)} %get-tuple-element.31) | copy-start | bytes 6148
  103.2 234.7 %reduce-scatter.5.cloned.1.call-start = ((), (), s32[]{:S(2)}) async-start(), calls=%async_computation.3 | async-start | bytes 4587520 | tf_op jit(solution)/shard_map/reduce_scatter | solution.py:163
  145.8 110.3 %copy-start.11 = (f32[3584]{0:T(1024)S(1)}, f32[3584]{0:T(1024)}, u32[]{:S(2)}) copy-start(f32[3584]{0:T(1024)} %reduce.4) | copy-start | bytes 43012
  145.8 110.3 %copy-start.34 = (bf16[1,3584,128]{2,1,0:T(8,128)(2,1)S(1)}, bf16[1,3584,128]{2,1,0:T(8,128)(2,1)}, u32[]{:S(2)}) copy-start(bf16[1,3584,128]{2,1,0:T(8,128)(2,1)} %param.24) | copy-start | bytes 2752516
  145.8 110.3 %copy-start.36 = (f32[1,128]{1,0:T(1,128)S(1)}, f32[1,128]{1,0:T(1,128)}, u32[]{:S(2)}) copy-start(f32[1,128]{1,0:T(1,128)} %param.25) | copy-start | bytes 1540
  147.8 23.8 %collective-permute-start.3 = (bf16[128,3584]{1,0:T(8,128)(2,1)S(1)}, bf16[128,3584]{1,0:T(8,128)(2,1)S(1)}, u32[]{:S(2)}, u32[]{:S(2)}) collective-permute-start(bf16[128,3584]{1,0:T(8,128)(2,1)S(1)} %bitcast_select_fusion.2), channel_id=1, source_target_pairs={{0,1},{1,2},{2,3},{3,0},{4,5},{5,6},{6,7},{7,4},{8,9},{9,10},{10,1... | collective-permute-start | bytes 2752520 | tf_op jit(solution)/shard_map/ppermute | solution.py:20
  148.6 23.1 %collective-permute-start.5 = (bf16[128,3584]{1,0:T(8,128)(2,1)S(1)}, bf16[128,3584]{1,0:T(8,128)(2,1)S(1)}, u32[]{:S(2)}, u32[]{:S(2)}) collective-permute-start(bf16[128,3584]{1,0:T(8,128)(2,1)S(1)} %bitcast_select_fusion.2), channel_id=1, source_target_pairs={{0,3},{1,0},{2,1},{3,2},{4,7},{5,4},{6,5},{7,6},{8,11},{9,8},{10,9... | collective-permute-start | bytes 2752520 | tf_op jit(solution)/shard_map/ppermute | solution.py:22
  171.7 22.5 %collective-permute-start.4 = (bf16[128,3584]{1,0:T(8,128)(2,1)S(1)}, bf16[128,3584]{1,0:T(8,128)(2,1)S(1)}, u32[]{:S(2)}, u32[]{:S(2)}) collective-permute-start(bf16[128,3584]{1,0:T(8,128)(2,1)S(1)} %collective-permute-done.3), channel_id=1, source_target_pairs={{0,1},{1,2},{2,3},{3,0},{4,5},{5,6},{6,7},{7,4},{8,9},{9,10},{10,1... | collective-permute-start | bytes 2752520 | tf_op jit(solution)/shard_map/ppermute | solution.py:20
  209.5 48.1 %copy-start.16 = (f32[64]{0:T(128)S(1)}, f32[64]{0:T(128)}, u32[]{:S(2)}) copy-start(f32[64]{0:T(128)} %multiply_power_fusion) | copy-start | bytes 772
  209.5 49.3 %copy-start.21 = (f32[896]{0:T(1024)S(1)}, f32[896]{0:T(1024)}, u32[]{:S(2)}) copy-start(f32[896]{0:T(1024)} %reduce.5) | copy-start | bytes 10756
  209.6 49.3 %slice-start.2 = ((s8[6422528]{0:T(1024)(128)(4,1)}), s8[4194304]{0:T(1024)(128)(4,1)S(1)}, s32[]{:S(2)}) async-start(s8[6422528]{0:T(1024)(128)(4,1)} %bitcast.171), calls=%async_computation.6 | async-start | bytes 8388608
  209.6 45.7 %collective-permute-start.6 = (bf16[512,3584]{1,0:T(8,128)(2,1)S(1)}, bf16[512,3584]{1,0:T(8,128)(2,1)S(1)}, u32[]{:S(2)}, u32[]{:S(2)}) collective-permute-start(bf16[512,3584]{1,0:T(8,128)(2,1)S(1)} %fusion.36), channel_id=1, source_target_pairs={{124,0},{0,4},{4,8},{8,12},{12,16},{16,20},{20,24},{24,28},{28,32}... | collective-permute-start | bytes 11010056 | tf_op jit(solution)/shard_map/ppermute | solution.py:30
  255.3 3.5 copy-start.4
  256.1 2.7 slice-start.3
  274.4 7.6 %copy-start.12 = (f32[3584]{0:T(1024)S(1)}, f32[3584]{0:T(1024)}, u32[]{:S(2)}) copy-start(f32[3584]{0:T(1024)} %reduce.4) | copy-start | bytes 43012
  274.4 7.6 %copy-start.38 = (f32[1,128]{1,0:T(1,128)S(1)}, f32[1,128]{1,0:T(1,128)}, u32[]{:S(2)}) copy-start(f32[1,128]{1,0:T(1,128)} %param.27) | copy-start | bytes 1540
  277.4 3.0 copy-start.1
  290.5 47.5 %copy-start.6 = (bf16[2,128,3584]{2,1,0:T(8,128)(2,1)S(1)}, bf16[2,128,3584]{2,1,0:T(8,128)(2,1)}, u32[]{:S(2)}) copy-start(bf16[2,128,3584]{2,1,0:T(8,128)(2,1)} %param.19) | copy-start | bytes 5505028
  299.6 99.5 %copy-start.32 = (s32[1,3]{1,0:T(1,128)S(1)}, s32[1,3]{1,0:T(1,128)}, u32[]{:S(2)}) copy-start(s32[1,3]{1,0:T(1,128)} %param.18) | copy-start | bytes 40
  299.6 159.0 %copy-start.13 = (s32[1,3]{1,0:T(1,128)S(1)}, s32[1,3]{1,0:T(1,128)}, u32[]{:S(2)}) copy-start(s32[1,3]{1,0:T(1,128)} %param.17) | copy-start | bytes 40
  299.6 159.0 %copy-start.18 = (s32[3]{0:T(128)S(1)}, s32[3]{0:T(128)}, u32[]{:S(2)}) copy-start(s32[3]{0:T(128)} %copy-done.17) | copy-start | bytes 40
  299.6 159.0 %copy-start.19 = (s32[1024]{0:T(1024)S(1)}, s32[1024]{0:T(1024)}, u32[]{:S(2)}) copy-start(s32[1024]{0:T(1024)} %param.29) | copy-start | bytes 12292
  299.6 159.2 %copy-start.27 = (s32[3]{0:T(128)S(1)}, s32[3]{0:T(128)}, u32[]{:S(2)}) copy-start(s32[3]{0:T(128)} %copy-done.26) | copy-start | bytes 40
  299.7 159.2 %copy-start.29 = (s32[3]{0:T(128)S(1)}, s32[3]{0:T(128)}, u32[]{:S(2)}) copy-start(s32[3]{0:T(128)} %copy-done.28) | copy-start | bytes 40
  299.7 159.3 %copy-start.23 = (s32[3]{0:T(128)S(1)}, s32[3]{0:T(128)}, u32[]{:S(2)}) copy-start(s32[3]{0:T(128)} %copy-done.22) | copy-start | bytes 40
  299.7 159.4 %copy-start.25 = (s32[3]{0:T(128)S(1)}, s32[3]{0:T(128)}, u32[]{:S(2)}) copy-start(s32[3]{0:T(128)} %copy-done.24) | copy-start | bytes 40
  339.8 119.4 %copy-start.7 = (bf16[128,3584]{1,0:T(8,128)(2,1)S(1)}, bf16[128,3584]{1,0:T(8,128)(2,1)}, u32[]{:S(2)}) copy-start(bf16[128,3584]{1,0:T(8,128)(2,1)} %reduce-scatter.3.cloned.1.call-done) | copy-start | bytes 2752516
  339.8 121.1 %copy-start.8 = (bf16[128,3584]{1,0:T(8,128)(2,1)S(1)}, bf16[128,3584]{1,0:T(8,128)(2,1)}, u32[]{:S(2)}) copy-start(bf16[128,3584]{1,0:T(8,128)(2,1)} %reduce-scatter.5.cloned.1.call-done) | copy-start | bytes 2752516
  339.8 23.6 %collective-permute-start.8 = (bf16[128,3584]{1,0:T(8,128)(2,1)S(1)}, bf16[128,3584]{1,0:T(8,128)(2,1)S(1)}, u32[]{:S(2)}, u32[]{:S(2)}) collective-permute-start(bf16[128,3584]{1,0:T(8,128)(2,1)S(1)} %bitcast_select_fusion.3), channel_id=1, source_target_pairs={{0,1},{1,2},{2,3},{3,0},{4,5},{5,6},{6,7},{7,4},{8,9},{9,10},{10,1... | collective-permute-start | bytes 2752520 | tf_op jit(solution)/shard_map/ppermute | solution.py:20
  340.3 23.1 %collective-permute-start.10 = (bf16[128,3584]{1,0:T(8,128)(2,1)S(1)}, bf16[128,3584]{1,0:T(8,128)(2,1)S(1)}, u32[]{:S(2)}, u32[]{:S(2)}) collective-permute-start(bf16[128,3584]{1,0:T(8,128)(2,1)S(1)} %bitcast_select_fusion.3), channel_id=1, source_target_pairs={{0,3},{1,0},{2,1},{3,2},{4,7},{5,4},{6,5},{7,6},{8,11},{9,8},{10,9... | collective-permute-start | bytes 2752520 | tf_op jit(solution)/shard_map/ppermute | solution.py:22
  363.5 22.5 %collective-permute-start.9 = (bf16[128,3584]{1,0:T(8,128)(2,1)S(1)}, bf16[128,3584]{1,0:T(8,128)(2,1)S(1)}, u32[]{:S(2)}, u32[]{:S(2)}) collective-permute-start(bf16[128,3584]{1,0:T(8,128)(2,1)S(1)} %collective-permute-done.8), channel_id=1, source_target_pairs={{0,1},{1,2},{2,3},{3,0},{4,5},{5,6},{6,7},{7,4},{8,9},{9,10},{10,1... | collective-permute-start | bytes 2752520 | tf_op jit(solution)/shard_map/ppermute | solution.py:20
  399.1 203.3 %collective-permute-start.11 = (bf16[512,3584]{1,0:T(8,128)(2,1)}, bf16[512,3584]{1,0:T(8,128)(2,1)}, u32[]{:S(2)}, u32[]{:S(2)}) collective-permute-start(bf16[512,3584]{1,0:T(8,128)(2,1)} %fusion.29), channel_id=1, source_target_pairs={{124,0},{0,4},{4,8},{8,12},{12,16},{16,20},{20,24},{24,28},{28,32}... | collective-permute-start | bytes 11010056 | tf_op jit(solution)/shard_map/ppermute | solution.py:30
  399.1 45.9 %collective-permute-start.12 = (s32[3]{0:T(128)S(1)}, s32[3]{0:T(128)S(1)}, u32[]{:S(2)}, u32[]{:S(2)}) collective-permute-start(s32[3]{0:T(128)S(1)} %fusion.129), channel_id=1, source_target_pairs={{124,0},{0,4},{4,8},{8,12},{12,16},{16,20},{20,24},{24,28},{28,32}... | collective-permute-start | bytes 44 | tf_op jit(solution)/shard_map/ppermute | solution.py:30
Sparse Core Ops, SparseCore 0:
  103.3 42.4 reduce-scatter.2
  299.8 38.0 reduce-scatter.4
